TPU v7x, 256 devices: a whole 4x4x8 slice. The times are simulated.
256 devices in a mesh: row: 16 (over y, z_hi), col: 16 (over x, z_lo, core).
Axes of the slice: x: 4, y: 4, z: 8 (z_hi: 4, z_lo: 2; z = z_hi * 2 + z_lo), core: 2. Of those that a mesh axis runs over, the one named last changes fastest.
Arguments:
- object_field: float32 [2, 6144, 6144], P(None, 'row', 'col'), may hold values from -6 to 6
- probe: float32 [4, 2, 128, 128], replicated, may hold values from -6 to 6
- positions: int32 [16, 16, 8, 2], P('row', 'col'), may hold values from 0 to 383
- counts: int32 [16, 16], P('row', 'col'), may hold values from 4 to 8, as said below
- measured: float32 [16, 16, 8, 128, 128], P('row', 'col'), may hold values from 0 to 3
Outputs:
- object_grad: float32 [2, 6144, 6144], P(None, 'row', 'col')
- probe_grad: float32 [4, 2, 128, 128], replicated
Inputs may be any that keep to these rules, and one draw needn't show every extreme that they name: `counts`: devices in the first or last index of either axis hold between 4 and 8 live slots; all other devices hold 8.
All inputs are finite; a program needn't handle non-finite values.
Results may differ from a plain program's by a relative error of at most 0.00016.
Values sent between devices are 32-bit elements; how exact they have to be, the bound alone decides.
A program may use at most 64 MiB of HBM per device.

v0:
```python
import functools
import math

import jax
import jax.numpy as jnp
import numpy as np
from jax import lax
from jax.experimental import pallas as pl
from jax.experimental.pallas import tpu as pltpu
from jax.sharding import PartitionSpec as P

MESH = pl.DeviceIdType.MESH
UNROLL = 4
VLIM = 60
PIECES = 8
RELEASE = (1, 1, 1, 1, 2, 1)
ANY = pl.BlockSpec(memory_space=pl.ANY)
VMEM = pl.BlockSpec(memory_space=pltpu.VMEM)
INSPEC = ANY
SMEM = pl.BlockSpec(memory_space=pltpu.SMEM)
F32 = jnp.float32
BF16 = jnp.bfloat16
N = 128
HALF = 64
SIDES = ((-1, 0), (1, 0), (0, -1), (0, 1), (-1, -1), (-1, 1), (1, -1), (1, 1))
OPPOSITE = tuple(SIDES.index((-a, -b)) for a, b in SIDES)


def neighbours(rows, cols):
    r, c = lax.axis_index("row"), lax.axis_index("col")
    out = []
    for dr, dc in SIDES:
        there = True
        if dr:
            there = (r > 0) if dr < 0 else (r < rows - 1)
        if dc:
            col_there = (c > 0) if dc < 0 else (c < cols - 1)
            there = col_there if there is True else jnp.logical_and(there, col_there)
        out.append((there, (r + dr, c + dc)))
    return out


def pack_low(tile):
    k = tile.shape[1] // 2
    lane = lax.broadcasted_iota(jnp.int32, (2, k, N), 2)
    return jnp.where(lane < HALF, tile[:, :k], pltpu.roll(tile[:, k:], HALF, 2))


def pack_high(tile):
    k = tile.shape[1] // 2
    lane = lax.broadcasted_iota(jnp.int32, (2, k, N), 2)
    return jnp.where(lane < HALF, pltpu.roll(tile[:, :k], HALF, 2), tile[:, k:])


def tables():
    ramp = np.arange(N)
    angles = 2.0 * math.pi / N * (ramp[:, None] * ramp[None, :] % N)
    cos, sin = np.cos(angles) / math.sqrt(N), np.sin(angles) / math.sqrt(N)
    minus = np.block([[cos, -sin], [sin, cos]]).astype(np.float32)
    return np.stack([minus, minus.T])


def each(count, body, unroll):
    def some(i, carry):
        for k in range(unroll):
            body(i * unroll + k)
        return carry

    lax.fori_loop(0, count // unroll, some, 0)


def split(x):
    high = x.astype(BF16)
    return high, (x - high.astype(F32)).astype(BF16)


def dot(a, b):
    return jnp.dot(a, b, preferred_element_type=F32)


def times_table(x, high, low):
    x_high, x_low = split(x)
    return dot(x_high, high) + (dot(x_low, high) + dot(x_high, low))


def table_times(high, low, x):
    x_high, x_low = split(x)
    return dot(high, x_high) + (dot(high, x_low) + dot(low, x_high))


def peers():
    r, c = lax.axis_index("row"), lax.axis_index("col")
    y, z_hi = r // 4, r % 4
    x, z_lo, core = c // 4, c // 2 % 2, c % 2
    plane = [((y + k // 4) % 4 * 4 + z_hi, (x + k % 4) % 4 * 4 + c % 4) for k in range(1, 16)]
    z = z_hi * 2 + z_lo
    along_z = []
    for k in range(1, 8):
        other = (z + k) % 8
        along_z.append((y * 4 + other // 2, x * 4 + other % 2 * 2 + core))
    return x, y, z, core, plane, along_z, (r, c + 1 - 2 * core)


def remote(src, dst, send_sem, recv_sem, device):
    return pltpu.make_async_remote_copy(
        src_ref=src, dst_ref=dst, send_sem=send_sem, recv_sem=recv_sem, device_id=device, device_id_type=MESH)


def sum_everywhere(ring, total, full, from_core, in_xy, in_z, send_sem, recv_sem, scale):
    x, y, z, core, plane, along_z, sibling = ring
    rows = total.shape[0]
    half, piece = rows // 2, rows // 32
    mine = core * half
    own = mine + (y * 4 + x) * piece
    used = [0]

    def send(src, dst, device):
        i = used[0]
        used[0] += 1
        copy = remote(src, dst, send_sem.at[i], recv_sem.at[i], device)
        copy.start()
        return copy

    def finish(copies):
        for copy in copies:
            copy.wait()

    span = lambda start, count: pl.ds(pl.multiple_of(start, 8), count)
    at = lambda ref, start, count: ref.at[span(start, count), :]

    def steps():
        copies = [send(at(total, half - mine, half), from_core, sibling)]
        yield
        finish(copies)
        total[span(mine, half), :] += from_core[...]
        copies = [send(at(total, mine + ((y + k // 4) % 4 * 4 + (x + k % 4) % 4) * piece, piece), in_xy.at[k - 1],
                       plane[k - 1]) for k in range(1, 16)]
        yield
        finish(copies)
        in_z[z] = total[span(own, piece), :] + sum(in_xy[k] for k in range(15))
        copies = [send(in_z.at[z], in_z.at[z], device) for device in along_z]
        yield
        finish(copies)
        full[span(own, piece), :] = sum(in_z[k] for k in range(8)) * scale
        copies = [send(at(full, own, piece), at(full, own, piece), device) for device in plane]
        yield
        finish(copies)
        copies = [send(at(full, mine, half), at(full, mine, half), sibling)]
        yield
        finish(copies)
        yield

    run = steps()
    return lambda: next(run)


def spread(x, k):
    return x, pltpu.roll(x, HALF, 2)


def turn_lanes(x, by):
    lane = lax.broadcasted_iota(jnp.int32, (8 * x.shape[0], N), 1)
    return jnp.take_along_axis(x.reshape(-1, N), (lane + (N - by)) & (N - 1), axis=1).reshape(x.shape)


def turn_rows(x, by):
    index = (lax.broadcasted_iota(jnp.int32, (8, N), 0) + (8 - by)) & 7
    return jnp.stack([jnp.take_along_axis(x[k], index, axis=0) for k in range(x.shape[0])])


def kernel(rows, cols, scale, pos_in, count_in, obj, probe_in, measured_in, table_in, out, full,
           pos, count, ext, field, probe, measured, table_whole, table, patches, mids, sums, strips, strips_in, corners, corners_in,
           moved, rim_sides, rim_corners, land_up, land_down, land_sides, land_corners,
           total, from_core, in_xy, in_z, load_sem, halo_send, halo_recv, rim_send, rim_recv, send_sem, recv_sem):
    modes, slots = probe.shape[0], measured.shape[0]
    size = out.shape[1]
    tiles = size // N + 2
    edge, far_edge = HALF // 8, (HALF + size) // 8
    groups = N // 8
    near = neighbours(rows, cols)

    loads = [pltpu.make_async_copy(a, b, load_sem.at[i]) for i, (a, b) in enumerate((
        (obj, ext.at[:, pl.ds(edge, size // 8), :, pl.ds(N, size)]),
        (pos_in, pos), (count_in, count), (probe_in, probe), (measured_in, measured), (table_in, table_whole)))]
    for load in loads:
        load.start()

    barrier = pltpu.get_barrier_semaphore()
    ring = peers()
    others = ring[-3] + ring[-2] + [ring[-1]]
    for device in others:
        pl.semaphore_signal(barrier, inc=1, device_id=device, device_id_type=MESH)
    for there, device in near:
        @pl.when(there)
        def _():
            pl.semaphore_signal(barrier, inc=1, device_id=device, device_id_type=MESH)
    pl.semaphore_wait(barrier, len(others) + sum(there.astype(jnp.int32) for there, _ in near))

    sources = [obj.at[:, pl.ds(0, edge)], obj.at[:, pl.ds(size // 8 - edge, edge)],
               strips.at[0], strips.at[1]] + [corners.at[i] for i in range(4)]
    landing = [ext.at[:, pl.ds(0, edge), :, pl.ds(N, size)], ext.at[:, pl.ds(far_edge, edge), :, pl.ds(N, size)],
               strips_in.at[0], strips_in.at[1]] + [corners_in.at[i] for i in range(4)]
    halo = [remote(sources[i], landing[OPPOSITE[i]], halo_send.at[i], halo_recv.at[OPPOSITE[i]], near[i][1])
            for i in range(8)]

    def start(copies, side):
        @pl.when(near[side][0])
        def _():
            copies[side].start()

    start(halo, 0)
    start(halo, 1)
    loads[0].wait()
    first_tile = ext[:, edge:far_edge, :, N:2 * N].reshape(2, size, N)
    last_tile = ext[:, edge:far_edge, :, size:size + N].reshape(2, size, N)
    strips[0] = pack_low(first_tile)
    start(halo, 2)
    strips[1] = pack_high(last_tile)
    start(halo, 3)
    corners[0] = pack_low(first_tile[:, :HALF])
    corners[1] = pack_high(last_tile[:, :HALF])
    corners[2] = pack_low(first_tile[:, size - HALF:])
    corners[3] = pack_high(last_tile[:, size - HALF:])
    for side in range(4, 8):
        start(halo, side)
    total[...] = jnp.zeros_like(total)
    for g in (0, groups + 2):
        moved[:, :, g] = jnp.zeros((slots, 2, 8, size + 2 * N), F32)
    for load in loads[1:]:
        load.wait()
    table[0], table[1] = split(table_whole[0])
    table[2], table[3] = split(table_whole[1])
    for side in range(8):
        @pl.when(jnp.logical_not(near[side][0]))
        def _():
            landing[side][...] = jnp.zeros(landing[side].shape, F32)
    for t in range(1, tiles - 1):
        field[:, t, edge:far_edge] = ext[:, edge:far_edge, :, t * N:(t + 1) * N]
    for side in range(8):
        @pl.when(near[side][0])
        def _():
            halo[side].wait_send()
            halo[OPPOSITE[side]].wait_recv()

    def unpack(packed, at, lane, is_low):
        k = packed.shape[1] // 8
        as_is, turned = spread(packed, k)
        first, second = (as_is, turned) if is_low else (turned, as_is)
        field[:, lane // N, at:at + k] = first.reshape(2, k, 8, N)
        field[:, lane // N, at + k:at + 2 * k] = second.reshape(2, k, 8, N)

    unpack(strips_in[0], edge, 0, False)
    unpack(strips_in[1], edge, N + size, True)
    unpack(corners_in[0], 0, 0, False)
    unpack(corners_in[1], 0, N + size, True)
    unpack(corners_in[2], far_edge, 0, False)
    unpack(corners_in[3], far_edge, N + size, True)

    for t in range(1, tiles - 1):
        field[:, t, :edge] = ext[:, :edge, :, t * N:(t + 1) * N]
        field[:, t, far_edge:] = ext[:, far_edge:, :, t * N:(t + 1) * N]

    minus_high, minus_low, plus_high, plus_low = (table[i] for i in range(4))
    lane = lax.broadcasted_iota(jnp.int32, (groups + 1, 8, N), 2)
    step = lax.broadcasted_iota(jnp.int32, (groups + 1, 8, N), 1)
    live = count[0, 0]

    def place(slot):
        row, col = pos[0, slot], pos[1, slot] + HALF
        return row // 8, row % 8, col // N, col % N

    def one_slot(slot):
        group, down_by, tile, shift = place(slot)
        kept = lane >= shift

        def cut(part):
            a, b = (jnp.stack([field[part, tile + t, group + k] for k in range(groups + 1)]) for t in (0, 1))
            x = turn_lanes(jnp.where(kept, a, b), N - shift)
            x = turn_rows(x, 8 - down_by)
            return jnp.where(step[:groups] < 8 - down_by, x[:groups], x[1:]).reshape(N, N)

        p_re, p_im = cut(0), cut(1)
        patches[slot, 0] = p_re
        patches[slot, 1] = p_im
        waves = []
        for m in range(modes):
            q_re, q_im = probe[m, 0], probe[m, 1]
            waves.append(jnp.concatenate([q_re * p_re - q_im * p_im, q_re * p_im + q_im * p_re], axis=1))
        half = times_table(jnp.concatenate(waves, axis=0), minus_high, minus_low)
        half = jnp.concatenate(
            [jnp.concatenate([half[m * N:(m + 1) * N, :N], half[m * N:(m + 1) * N, N:]], axis=0)
             for m in range(modes)], axis=1)
        far = table_times(plus_high, plus_low, half)
        power = far[:N] * far[:N] + far[N:] * far[N:]
        intensity = sum(power[:, m * N:(m + 1) * N] for m in range(modes))
        alive = jnp.where(slot < live, 1.0, 0.0).astype(F32)
        factor = (1.0 - measured[slot] * lax.rsqrt(intensity + 0.1)) * alive
        wide = jnp.concatenate([factor] * modes, axis=1)
        far = far * jnp.concatenate([wide, wide], axis=0)
        half = table_times(minus_high, minus_low, far)
        for m in range(modes):
            mids[slot, m, :, :N] = half[:N, m * N:(m + 1) * N]
            mids[slot, m, :, N:] = half[N:, m * N:(m + 1) * N]

    each(slots, one_slot, UNROLL)

    def last_step(slot, some):
        g = times_table(mids[slot, some[0]:some[-1] + 1].reshape(-1, 2 * N), plus_high, plus_low)
        p_re, p_im = patches[slot, 0], patches[slot, 1]
        o_re = jnp.zeros((N, N), F32)
        o_im = jnp.zeros((N, N), F32)
        for k, m in enumerate(some):
            g_re, g_im = g[k * N:(k + 1) * N, :N], g[k * N:(k + 1) * N, N:]
            q_re, q_im = probe[m, 0], probe[m, 1]
            o_re += q_re * g_re + q_im * g_im
            o_im += q_re * g_im - q_im * g_re
            total[2 * m * N:(2 * m + 1) * N] += p_re * g_re + p_im * g_im
            total[(2 * m + 1) * N:(2 * m + 2) * N] += p_re * g_im - p_im * g_re
        return o_re, o_im

    def first_modes(slot):
        sums[slot, 0], sums[slot, 1] = last_step(slot, early)

    def last_modes(slot):
        _, down_by, tile, shift = place(slot)
        o_re, o_im = last_step(slot, late)
        blank = jnp.zeros((1, 8, N), F32)
        for part, value in ((0, sums[slot, 0] + o_re), (1, sums[slot, 1] + o_im)):
            x = turn_lanes(value.reshape(groups, 8, N), shift)
            x = turn_rows(x, down_by)
            x = jnp.where(step >= down_by, jnp.concatenate([x, blank]), jnp.concatenate([blank, x]))
            for t in range(tiles):
                from_start = lane[:1] + (t * N - shift) - tile * N
                inside = jnp.logical_and(from_start >= 0, from_start < N)
                moved[slot, part, 1:groups + 2, :, t * N:(t + 1) * N] = jnp.where(inside, x, 0.0)

    early, late = tuple(range(modes // 2)), tuple(range(modes // 2, modes))
    cut_at = 2 * len(early) * N
    advance_a, advance_b = (
        sum_everywhere(ring, total.at[rows_of], full.at[rows_of], from_core.at[i], in_xy.at[i], in_z.at[i],
                       send_sem.at[i], recv_sem.at[i], scale)
        for i, rows_of in enumerate((pl.ds(0, cut_at), pl.ds(cut_at, total.shape[0] - cut_at))))
    each(slots, first_modes, UNROLL)
    advance_a()
    each(slots, last_modes, UNROLL)
    advance_a()
    advance_b()
    starts = [place(slot)[0] for slot in range(slots)]

    def gather(g):
        at = [jnp.clip(g - start + 1, 0, groups + 2) for start in starts]
        for part in (0, 1):
            ext[part, g] = sum(moved[slot, part, at[slot]] for slot in range(slots))

    each(ext.shape[1], gather, 1)
    advance_b()
    block = lambda at, k, lane: ext[:, at:at + k, :, lane:lane + N].reshape(2, 8 * k, N)
    rim_sides[0] = pack_high(block(edge, size // 8, 0))
    rim_sides[1] = pack_low(block(edge, size // 8, N + size))
    rim_corners[0] = pack_high(block(0, edge, 0))
    rim_corners[1] = pack_low(block(0, edge, N + size))
    rim_corners[2] = pack_high(block(far_edge, edge, 0))
    rim_corners[3] = pack_low(block(far_edge, edge, N + size))

    per_row, per_side = edge // PIECES, size // 2 // PIECES
    rims = []
    for p in range(PIECES):
        rows_of, part_of = pl.ds(p * per_row, per_row), pl.ds(p * per_side, per_side)
        rims.append([
            (0, ext.at[:, rows_of, :, pl.ds(N, size)], land_down.at[:, rows_of]),
            (1, ext.at[:, pl.ds(far_edge + p * per_row, per_row), :, pl.ds(N, size)], land_up.at[:, rows_of]),
            (2, rim_sides.at[0, :, part_of], land_sides.at[1, :, part_of]),
            (3, rim_sides.at[1, :, part_of], land_sides.at[0, :, part_of])])
    for i in range(4):
        rims[i * PIECES // 4].append((4 + i, rim_corners.at[i], land_corners.at[OPPOSITE[4 + i] - 4]))
    rims = [[(side, remote(src, dst, rim_send.at[p, side], rim_recv.at[p, OPPOSITE[side]], near[side][1]))
             for side, src, dst in piece] for p, piece in enumerate(rims)]
    left = list(rims)

    def release(count):
        for _ in range(min(count, len(left))):
            for side, copy in left.pop(0):
                @pl.when(near[side][0])
                def _():
                    copy.start()

    release(RELEASE[0])
    advance_a()
    release(RELEASE[1])
    out[...] = ext[:, edge:far_edge, :, N:N + size].reshape(2, size, size)
    advance_b()
    release(RELEASE[2])
    advance_a()
    release(RELEASE[3])
    advance_b()
    release(RELEASE[4])
    advance_a()
    release(RELEASE[5])
    advance_b()
    release(PIECES)
    advance_a()
    advance_b()

    def add(packed, row, is_low):
        k = packed.shape[1]
        lane_of = lax.broadcasted_iota(jnp.int32, (2, k, N), 2)
        as_is, turned = spread(packed, k)
        first, second = (as_is, turned) if is_low else (turned, as_is)
        inside = (lane_of < HALF) if is_low else (lane_of >= HALF)
        at = 0 if is_low else size - N
        out[:, row:row + k, at:at + N] += jnp.where(inside, first, 0.0)
        out[:, row + k:row + 2 * k, at:at + N] += jnp.where(inside, second, 0.0)

    for piece in rims:
        for side, copy in piece:
            @pl.when(near[side][0])
            def _():
                copy.wait_send()

            @pl.when(near[OPPOSITE[side]][0])
            def _():
                copy.wait_recv()

    for side in range(8):
        @pl.when(near[side][0])
        def _():
            if side == 0:
                out[:, :HALF, :] += land_up[...].reshape(2, HALF, size)
            elif side == 1:
                out[:, size - HALF:, :] += land_down[...].reshape(2, HALF, size)
            elif side < 4:
                add(land_sides[side - 2], 0, side == 2)
            else:
                add(land_corners[side - 4], 0 if side < 6 else size - HALF, side in (4, 6))


def local(rows, cols, object_field, probe, positions, counts, measured):
    size = object_field.shape[1]
    slots, modes = measured.shape[2], probe.shape[0]
    scale = 1.0 / math.sqrt(rows * cols * slots)
    height = 2 * modes * N
    vm = lambda *dims: pltpu.VMEM(dims, F32)
    dma = lambda *count: pltpu.SemaphoreType.DMA(count)
    strip, side, corner = (2, HALF // 8, 8, size), (2, 2, size // 2, N), (4, 2, HALF // 2, N)
    out, full = pl.pallas_call(
        functools.partial(kernel, rows, cols, scale),
        out_shape=[jax.ShapeDtypeStruct(object_field.shape, F32), jax.ShapeDtypeStruct((height, N), F32)],
        in_specs=[INSPEC] * 6,
        out_specs=[VMEM] * 2,
        scratch_shapes=[
            pltpu.SMEM((2, slots), jnp.int32), pltpu.SMEM(counts.shape, jnp.int32),
            vm(2, (size + N) // 8, 8, size + 2 * N), vm(2, size // N + 2, (size + N) // 8, 8, N), vm(*probe.shape), vm(slots, N, N),
            vm(2, 2 * N, 2 * N), pltpu.VMEM((4, 2 * N, 2 * N), BF16),
            vm(slots, 2, N, N), vm(slots, modes, N, 2 * N), vm(slots, 2, N, N),
            vm(*side), vm(*side), vm(*corner), vm(*corner),
            vm(slots, 2, N // 8 + 3, 8, size + 2 * N),
            vm(*side), vm(*corner),
            vm(*strip), vm(*strip), vm(*side), vm(*corner),
            vm(height, N), vm(2, height // 4, N), vm(2, 15, height // 64, N), vm(2, 8, height // 64, N),
            dma(6), dma(8), dma(8), dma(PIECES, 8), dma(PIECES, 8), dma(2, 39), dma(2, 39),
        ],
        compiler_params=pltpu.CompilerParams(
            collective_id=0, has_side_effects=True, vmem_limit_bytes=VLIM * 1024 * 1024),
        name="step",
    )(positions[0, 0].T, counts, object_field.reshape(2, size // 8, 8, size), probe, measured[0, 0], jnp.asarray(tables()))
    return out, full.reshape(probe.shape)


def solution(mesh):
    placed = (
        P(None, "row", "col"),
        P(),
        P("row", "col", None, None),
        P("row", "col"),
        P("row", "col", None, None, None),
    )
    return jax.shard_map(
        functools.partial(local, mesh.shape["row"], mesh.shape["col"]),
        mesh=mesh, in_specs=placed, out_specs=(P(None, "row", "col"), P()), check_vma=False)
```

profile of v0, /device:TPU:1, one launch (start us, length us, event | category | flops | bytes accessed | tf_op | source)
XLA Modules:
  0.0 74.8 jit_solution(7060203351879263501)
XLA Ops:
  1.3 70.3 %step.1 = (f32[2,384,384]{2,1,0:T(8,128)}, f32[1024,128]{1,0:T(8,128)}) custom-call(s32[2,8]{1,0:T(2,128)} %bitcast.9, s32[1,1]{1,0:T(1,128)S(6)} %copy.10.count_in, f32[2,48,8,384]{3,2,1,0:T(8,128)} %bitcast.6, f32[4,2,128,128]{3,2,1,0:T(8,128)} %probe_in.1, f32[8,128,128]{2,1,0:T(8,128)} %bitcast.8, f32[2,256,256]{2,1,0:T(8,128)} %constant.2.clone.table_in), custom_call_target="tpu_custom_call" | custom-call | tf_op jit(solution)/shard_map/step/pallas_call | solution.py:445
  71.6 0.0 copy-start
  71.6 2.4 %copy.11 = f32[2,384,384]{2,1,0:T(8,128)} copy(f32[2,384,384]{2,1,0:T(8,128)} %get-tuple-element.8) | data formatting | bytes 2359296
  74.0 0.0 copy-done
  74.0 0.8 %copy.12 = f32[4,2,128,128]{3,2,1,0:T(8,128)} copy(f32[4,2,128,128]{3,2,1,0:T(8,128)S(1)} %bitcast.7) | data formatting | bytes 1048576
Async XLA Ops:
  71.6 2.4 %copy-start = (f32[1024,128]{1,0:T(8,128)S(1)}, f32[1024,128]{1,0:T(8,128)}, u32[]{:S(2)}) copy-start(f32[1024,128]{1,0:T(8,128)} %get-tuple-element.5) | copy-start | bytes 1572868
where the time goes:
time: 75.7 us; the launch traced here: 74.8 us
  Pallas kernels  70.3 us (93%)
  local copies, waits for them, and re-layouts  3.21 us (4%)
  between operations  1.29 us (2%)
    pallas_call x1, Pallas kernels, local(): pl.pallas_call(functools.partial(kernel, rows, cols, scale), out_shape=[j...  70.3 us
    unnamed x4, local copies, waits for them, and re-layouts  3.21 us

commit v1 on v0

--- a/solution.py
+++ b/solution.py
@@ -13,6 +13,7 @@
 UNROLL = 4
 VLIM = 60
 PIECES = 8
+SHARES = 4
 RELEASE = (1, 1, 1, 1, 2, 1)
 ANY = pl.BlockSpec(memory_space=pl.ANY)
 VMEM = pl.BlockSpec(memory_space=pltpu.VMEM)
@@ -62,8 +63,7 @@
 
 def each(count, body, unroll):
     def some(i, carry):
-        for k in range(unroll):
-            body(i * unroll + k)
+        body([i * unroll + k for k in range(unroll)])
         return carry
 
     lax.fori_loop(0, count // unroll, some, 0)
@@ -85,7 +85,8 @@
 
 def table_times(high, low, x):
     x_high, x_low = split(x)
-    return dot(high, x_high) + (dot(high, x_low) + dot(low, x_high))
+    both = dot(jnp.concatenate([high, low], axis=0), x_high)
+    return both[:high.shape[0]] + (dot(high, x_low) + both[high.shape[0]:])
 
 
 def peers():
@@ -269,7 +270,7 @@
         row, col = pos[0, slot], pos[1, slot] + HALF
         return row // 8, row % 8, col // N, col % N
 
-    def one_slot(slot):
+    def waves_of(slot):
         group, down_by, tile, shift = place(slot)
         kept = lane >= shift
 
@@ -286,7 +287,14 @@
         for m in range(modes):
             q_re, q_im = probe[m, 0], probe[m, 1]
             waves.append(jnp.concatenate([q_re * p_re - q_im * p_im, q_re * p_im + q_im * p_re], axis=1))
-        half = times_table(jnp.concatenate(waves, axis=0), minus_high, minus_low)
+        return waves
+
+    def first_steps(some):
+        half = times_table(jnp.concatenate(sum((waves_of(slot) for slot in some), []), axis=0), minus_high, minus_low)
+        for k, slot in enumerate(some):
+            along_rows(slot, half[k * modes * N:(k + 1) * modes * N])
+
+    def along_rows(slot, half):
         half = jnp.concatenate(
             [jnp.concatenate([half[m * N:(m + 1) * N, :N], half[m * N:(m + 1) * N, N:]], axis=0)
              for m in range(modes)], axis=1)
@@ -302,37 +310,44 @@
             mids[slot, m, :, :N] = half[:N, m * N:(m + 1) * N]
             mids[slot, m, :, N:] = half[N:, m * N:(m + 1) * N]
 
-    each(slots, one_slot, UNROLL)
-
-    def last_step(slot, some):
-        g = times_table(mids[slot, some[0]:some[-1] + 1].reshape(-1, 2 * N), plus_high, plus_low)
-        p_re, p_im = patches[slot, 0], patches[slot, 1]
-        o_re = jnp.zeros((N, N), F32)
-        o_im = jnp.zeros((N, N), F32)
-        for k, m in enumerate(some):
-            g_re, g_im = g[k * N:(k + 1) * N, :N], g[k * N:(k + 1) * N, N:]
-            q_re, q_im = probe[m, 0], probe[m, 1]
-            o_re += q_re * g_re + q_im * g_im
-            o_im += q_re * g_im - q_im * g_re
-            total[2 * m * N:(2 * m + 1) * N] += p_re * g_re + p_im * g_im
-            total[(2 * m + 1) * N:(2 * m + 2) * N] += p_re * g_im - p_im * g_re
-        return o_re, o_im
-
-    def first_modes(slot):
-        sums[slot, 0], sums[slot, 1] = last_step(slot, early)
-
-    def last_modes(slot):
-        _, down_by, tile, shift = place(slot)
-        o_re, o_im = last_step(slot, late)
-        blank = jnp.zeros((1, 8, N), F32)
-        for part, value in ((0, sums[slot, 0] + o_re), (1, sums[slot, 1] + o_im)):
-            x = turn_lanes(value.reshape(groups, 8, N), shift)
-            x = turn_rows(x, down_by)
-            x = jnp.where(step >= down_by, jnp.concatenate([x, blank]), jnp.concatenate([blank, x]))
-            for t in range(tiles):
-                from_start = lane[:1] + (t * N - shift) - tile * N
-                inside = jnp.logical_and(from_start >= 0, from_start < N)
-                moved[slot, part, 1:groups + 2, :, t * N:(t + 1) * N] = jnp.where(inside, x, 0.0)
+    each(slots, first_steps, UNROLL)
+
+    def last_step(slots_now, some):
+        height = len(some) * N
+        x = [mids[slot, some[0]:some[-1] + 1].reshape(height, 2 * N) for slot in slots_now]
+        g_all = times_table(jnp.concatenate(x, axis=0), plus_high, plus_low)
+        result = []
+        for i, slot in enumerate(slots_now):
+            g = g_all[i * height:(i + 1) * height]
+            p_re, p_im = patches[slot, 0], patches[slot, 1]
+            o_re = jnp.zeros((N, N), F32)
+            o_im = jnp.zeros((N, N), F32)
+            for k, m in enumerate(some):
+                g_re, g_im = g[k * N:(k + 1) * N, :N], g[k * N:(k + 1) * N, N:]
+                q_re, q_im = probe[m, 0], probe[m, 1]
+                o_re += q_re * g_re + q_im * g_im
+                o_im += q_re * g_im - q_im * g_re
+                total[2 * m * N:(2 * m + 1) * N] += p_re * g_re + p_im * g_im
+                total[(2 * m + 1) * N:(2 * m + 2) * N] += p_re * g_im - p_im * g_re
+            result.append((o_re, o_im))
+        return result
+
+    def first_modes(some):
+        for slot, (o_re, o_im) in zip(some, last_step(some, early)):
+            sums[slot, 0], sums[slot, 1] = o_re, o_im
+
+    def last_modes(some):
+        for slot, (o_re, o_im) in zip(some, last_step(some, late)):
+            _, down_by, tile, shift = place(slot)
+            blank = jnp.zeros((1, 8, N), F32)
+            for part, value in ((0, sums[slot, 0] + o_re), (1, sums[slot, 1] + o_im)):
+                x = turn_lanes(value.reshape(groups, 8, N), shift)
+                x = turn_rows(x, down_by)
+                x = jnp.where(step >= down_by, jnp.concatenate([x, blank]), jnp.concatenate([blank, x]))
+                for t in range(tiles):
+                    from_start = lane[:1] + (t * N - shift) - tile * N
+                    inside = jnp.logical_and(from_start >= 0, from_start < N)
+                    moved[slot, part, 1:groups + 2, :, t * N:(t + 1) * N] = jnp.where(inside, x, 0.0)
 
     early, late = tuple(range(modes // 2)), tuple(range(modes // 2, modes))
     cut_at = 2 * len(early) * N
@@ -347,7 +362,8 @@
     advance_b()
     starts = [place(slot)[0] for slot in range(slots)]
 
-    def gather(g):
+    def gather(some):
+        g, = some
         at = [jnp.clip(g - start + 1, 0, groups + 2) for start in starts]
         for part in (0, 1):
             ext[part, g] = sum(moved[slot, part, at[slot]] for slot in range(slots))
@@ -432,6 +448,24 @@
                 add(land_sides[side - 2], 0, side == 2)
             else:
                 add(land_corners[side - 4], 0 if side < 6 else size - HALF, side in (4, 6))
+
+
+def hand_over_kernel(a, b, out_a, out_b, held_a, held_b, load_sem, store_sem):
+    part_a, part_b = a.shape[1] // SHARES, b.shape[0] // SHARES
+    loads, stores = [], []
+    for i in range(SHARES):
+        rows_a, rows_b = pl.ds(i * part_a, part_a), pl.ds(i * part_b, part_b)
+        loads.append(pltpu.make_async_copy(a.at[:, rows_a], held_a.at[:, rows_a], load_sem.at[0, i]))
+        loads.append(pltpu.make_async_copy(b.at[rows_b], held_b.at[rows_b], load_sem.at[1, i]))
+        stores.append(pltpu.make_async_copy(held_a.at[:, rows_a], out_a.at[:, rows_a], store_sem.at[0, i]))
+        stores.append(pltpu.make_async_copy(held_b.at[rows_b], out_b.at[rows_b], store_sem.at[1, i]))
+    for load in loads:
+        load.start()
+    for load, store in zip(loads, stores):
+        load.wait()
+        store.start()
+    for store in stores:
+        store.wait()
 
 
 def local(rows, cols, object_field, probe, positions, counts, measured):
@@ -463,6 +497,15 @@
             collective_id=0, has_side_effects=True, vmem_limit_bytes=VLIM * 1024 * 1024),
         name="step",
     )(positions[0, 0].T, counts, object_field.reshape(2, size // 8, 8, size), probe, measured[0, 0], jnp.asarray(tables()))
+    out, full = pl.pallas_call(
+        hand_over_kernel,
+        out_shape=[jax.ShapeDtypeStruct(out.shape, F32), jax.ShapeDtypeStruct(full.shape, F32)],
+        in_specs=[ANY] * 2,
+        out_specs=[ANY] * 2,
+        scratch_shapes=[vm(*out.shape), vm(*full.shape), dma(2, SHARES), dma(2, SHARES)],
+        compiler_params=pltpu.CompilerParams(vmem_limit_bytes=VLIM * 1024 * 1024),
+        name="hand_over",
+    )(out, full)
     return out, full.reshape(probe.shape)
 
 

time: 75.7 us -> 73.3 us (0.968)
  local copies, waits for them, and re-layouts: 3.21 us -> 0 us
    unnamed x4 -> x0, local copies, waits for them, and re-layouts: 3.21 us -> none
    pallas_call x0 -> x1, Pallas kernels: none -> 2.29 us  [local(): pl.pallas_call(hand_over_kernel, out_shape=[jax.ShapeDtypeStruct(out.shap...]
    pallas_call x1, Pallas kernels: 70.3 us -> 68.7 us  [local(): pl.pallas_call(functools.partial(kernel, rows, cols, scale), out_shape=[j...]
where the time goes in v1:
time: 73.3 us; the launch traced here: 72.3 us
  Pallas kernels  71 us (97%)
  between operations  1.29 us (2%)
    pallas_call x1, Pallas kernels, local(): pl.pallas_call(functools.partial(kernel, rows, cols, scale), out_shape=[j...  68.7 us
    pallas_call x1, Pallas kernels, local(): pl.pallas_call(hand_over_kernel, out_shape=[jax.ShapeDtypeStruct(out.shap...  2.29 us

profile of v1, /device:TPU:1, one launch (start us, length us, event | category | flops | bytes accessed | tf_op | source)
XLA Modules:
  0.0 72.3 jit_solution(1828171153229510017)
XLA Ops:
  1.3 68.7 %step.1 = (f32[2,384,384]{2,1,0:T(8,128)}, f32[1024,128]{1,0:T(8,128)}) custom-call(s32[2,8]{1,0:T(2,128)} %bitcast.8, s32[1,1]{1,0:T(1,128)S(6)} %copy.8.count_in, f32[2,48,8,384]{3,2,1,0:T(8,128)} %bitcast.6, f32[4,2,128,128]{3,2,1,0:T(8,128)} %probe_in.1, f32[8,128,128]{2,1,0:T(8,128)} %bitcast.7, f32[2,256,256]{2,1,0:T(8,128)} %constant.2.clone.table_in), custom_call_target="tpu_custom_call" | custom-call | tf_op jit(solution)/shard_map/step/pallas_call | solution.py:479
  70.0 2.3 %hand_over.1 = (f32[2,384,384]{2,1,0:T(8,128)}, f32[1024,128]{1,0:T(8,128)}) custom-call(f32[2,384,384]{2,1,0:T(8,128)} %get-tuple-element.6.a, f32[1024,128]{1,0:T(8,128)} %get-tuple-element.7.b), custom_call_target="tpu_custom_call" | custom-call | tf_op jit(solution)/shard_map/hand_over/pallas_call | solution.py:500

commit v2 on v1

--- a/solution.py
+++ b/solution.py
@@ -10,7 +10,7 @@
 from jax.sharding import PartitionSpec as P
 
 MESH = pl.DeviceIdType.MESH
-UNROLL = 4
+UNROLL = 8
 VLIM = 60
 PIECES = 8
 SHARES = 4

time: 73.3 us -> 73.1 us (level)
  no operation moved by 1% of the time
where the time goes in v2:
time: 73.1 us; the launch traced here: 72 us
  Pallas kernels  70.7 us (97%)
  between operations  1.29 us (2%)
    pallas_call x1, Pallas kernels, local(): pl.pallas_call(functools.partial(kernel, rows, cols, scale), out_shape=[j...  68.4 us
    pallas_call x1, Pallas kernels, local(): pl.pallas_call(hand_over_kernel, out_shape=[jax.ShapeDtypeStruct(out.shap...  2.29 us

profile of v2, /device:TPU:1, one launch (start us, length us, event | category | flops | bytes accessed | tf_op | source)
XLA Modules:
  0.0 72.0 jit_solution(13928473626394081185)
XLA Ops:
  1.3 68.4 %step.1 = (f32[2,384,384]{2,1,0:T(8,128)}, f32[1024,128]{1,0:T(8,128)}) custom-call(s32[2,8]{1,0:T(2,128)} %bitcast.8, s32[1,1]{1,0:T(1,128)S(6)} %copy.8.count_in, f32[2,48,8,384]{3,2,1,0:T(8,128)} %bitcast.6, f32[4,2,128,128]{3,2,1,0:T(8,128)} %probe_in.1, f32[8,128,128]{2,1,0:T(8,128)} %bitcast.7, f32[2,256,256]{2,1,0:T(8,128)} %constant.2.clone.table_in), custom_call_target="tpu_custom_call" | custom-call | tf_op jit(solution)/shard_map/step/pallas_call | solution.py:479
  69.7 2.3 %hand_over.1 = (f32[2,384,384]{2,1,0:T(8,128)}, f32[1024,128]{1,0:T(8,128)}) custom-call(f32[2,384,384]{2,1,0:T(8,128)} %get-tuple-element.6.a, f32[1024,128]{1,0:T(8,128)} %get-tuple-element.7.b), custom_call_target="tpu_custom_call" | custom-call | tf_op jit(solution)/shard_map/hand_over/pallas_call | solution.py:500
